TPU v7x, 512 devices: a whole 4x8x8 slice. The times are simulated.
512 devices in a mesh: ctx: 64 (over z, x, core), tp: 8 (over y).
Axes of the slice: x: 4, y: 8, z: 8, core: 2. Of those that a mesh axis runs over, the one named last changes fastest.
Arguments:
- queries: bfloat16 [32768, 4096], P('ctx', 'tp'), may hold values from -6 to 6
- keys: bfloat16 [32768, 4096], P('ctx', 'tp'), may hold values from -6 to 6
- values: bfloat16 [32768, 4096], P('ctx', 'tp'), may hold values from -6 to 6
- out_weight: bfloat16 [4096, 4096], P('tp', 'ctx'), may hold values from -0.09375 to 0.09375
Outputs:
- mixed: bfloat16 [32768, 4096], P(('ctx', 'tp'))
All inputs are finite; a program needn't handle non-finite values.
Results may differ from a plain program's by a relative error of at most 0.018.
Values may be sent and summed in bfloat16 or wider, within the bound.
No kernel may reach another device: no remote copies, remote signals or barrier semaphores. Data moves between devices by JAX's collectives and lax.ppermute only.
A program may use at most 64 MiB of HBM per device.

v0:
```python
import jax
import jax.numpy as jnp
from jax import lax
from jax.sharding import PartitionSpec as P

HD = 128


def prefix(part, axis, combine, identity):
    place = lax.axis_index(axis)
    gathered = lax.all_gather(part, axis)
    state = jnp.zeros_like(part) + jnp.asarray(identity, part.dtype)

    def one(step, state):
        return combine(state, lax.dynamic_index_in_dim(gathered, step, 0, False))

    return lax.fori_loop(0, place, one, state)


def add_states(earlier, later):
    return earlier + later


def on_device(queries, keys, values, out_weight):
    tok_rows = queries.shape[0]
    head_dim = HD
    heads_here = queries.shape[1] // head_dim
    block_len = min(tok_rows, 512)
    blocks = tok_rows // block_len
    shape = (blocks, block_len, heads_here, head_dim)
    q_blk = queries.reshape(shape)
    k_blk = keys.reshape(shape)
    v_blk = values.reshape(shape)
    block_state = jnp.einsum("nthd,nthe->nhde", k_blk, v_blk, preferred_element_type=jnp.float32)
    own_total = jnp.sum(block_state, axis=0)
    inside = jnp.cumsum(block_state, axis=0) - block_state
    zeros_state = jnp.zeros_like(own_total)
    before = prefix(own_total, "ctx", add_states, zeros_state)
    carried = (before[None] + inside).astype(jnp.bfloat16)
    causal = jnp.arange(block_len)[:, None] >= jnp.arange(block_len)[None, :]
    scores = jnp.einsum("nthd,nshd->nhts", q_blk, k_blk, preferred_element_type=jnp.float32)
    scores = jnp.where(causal[None, None], scores, 0.0).astype(jnp.bfloat16)
    intra = jnp.einsum("nhts,nshe->nthe", scores, v_blk, preferred_element_type=jnp.float32)
    inter = jnp.einsum("nthd,nhde->nthe", q_blk, carried, preferred_element_type=jnp.float32)
    attended = inter + intra
    normed = attended / jnp.sqrt(jnp.mean(attended * attended, axis=-1, keepdims=True) + 1e-06)
    normed = normed.astype(jnp.bfloat16).reshape(tok_rows, heads_here * head_dim)
    terms = jnp.dot(
        normed,
        lax.all_gather(out_weight, "ctx", axis=1, tiled=True),
        preferred_element_type=jnp.float32,
    )
    summed = lax.psum_scatter(terms.astype(jnp.bfloat16), "tp", scatter_dimension=0, tiled=True)
    return summed


def solution(mesh):
    placed = (P("ctx", "tp"), P("ctx", "tp"), P("ctx", "tp"), P("tp", "ctx"))
    return jax.shard_map(
        on_device, mesh=mesh, in_specs=placed, out_specs=P(("ctx", "tp"), None), check_vma=False
    )
```

profile of v0, /device:TPU:1, one launch (start us, length us, event | category | flops | bytes accessed | tf_op | source)
XLA Modules:
  0.0 274.9 jit_solution(6830236183896022547)
XLA Ops:
  6.5 0.0 copy-start
  6.5 0.0 all-gather.6.cloned.1.call-start
  6.5 1.3 copy.16
  7.9 1.3 copy.17
  9.1 1.0 fusion.14
  10.1 0.0 copy-start.1
  10.1 0.0 all-gather.6.cloned.1.call-update
  10.1 0.0 all-gather.4.cloned.1.call-start
  10.2 0.7 all-gather.4.cloned.1.call-update
  10.9 0.0 reduce-scatter.2.cloned.1.call-start
  10.9 0.1 iota_compare_fusion
  11.0 111.6 %all-gather.6.cloned.1.call-done = f32[256,128,128]{2,1,0:T(8,128)} async-done(((f32[4,128,128]{2,1,0:T(8,128)}), f32[256,128,128]{2,1,0:T(8,128)}) %all-gather.6.cloned.1.call-update) | async-done | bytes 16777232 | tf_op jit(solution)/shard_map/all_gather | solution.py:11
  122.6 1.0 while.10
  122.6 1.0 bitcast_add_fusion.2
  123.7 0.0 copy-done
  123.7 0.0 copy-done.1
  123.7 1.3 fusion.6
  125.0 2.6 multiply_reduce_fusion
  127.6 0.1 divide_convert_fusion
  127.7 79.9 %all-gather.4.cloned.1.call-done = bf16[512,4096]{0,1:T(8,128)(2,1)} async-done(((bf16[512,64]{0,1:T(8,128)(2,1)}), bf16[512,4096]{0,1:T(8,128)(2,1)}) %all-gather.4.cloned.1.call-update) | async-done | bytes 4194320 | tf_op jit(solution)/shard_map/all_gather | solution.py:50
  207.6 6.5 %convolution_convert_fusion = bf16[512,4096]{1,0:T(8,128)(2,1)} fusion(bf16[512,512]{0,1:T(8,128)(2,1)S(1)} %bitcast.44, bf16[512,4096]{0,1:T(8,128)(2,1)} %all-gather.4.cloned.1.call-done), kind=kOutput, calls=%fused_computation.1 | convolution fusion | flops 2149580800 | bytes 8912896 | tf_op jit(solution)/shard_map/dot_general | solution.py:48
  214.1 0.0 reduce-scatter.2.cloned.1.call-update
  214.1 54.2 %reduce-scatter.2.cloned.1.call-done = bf16[64,4096]{1,0:T(8,128)(2,1)} async-done(((bf16[512,4096]{1,0:T(8,128)(2,1)}), bf16[64,4096]{1,0:T(8,128)(2,1)}) %reduce-scatter.2.cloned.1.call-update) | async-done | bytes 524304 | tf_op jit(solution)/shard_map/reduce_scatter | solution.py:53
  (2 shorter events, 0.0 us)
Async XLA Ops:
  6.5 117.1 %copy-start = (bf16[512,512]{1,0:T(8,128)(2,1)S(1)}, bf16[512,512]{1,0:T(8,128)(2,1)}, u32[]{:S(2)}) copy-start(bf16[512,512]{1,0:T(8,128)(2,1)} %param.6) | copy-start | bytes 1572868
  6.5 116.1 %all-gather.6.cloned.1.call-start = ((), (), s32[]{:S(2)}) async-start(), calls=%async_computation.3 | async-start | bytes 17039360 | tf_op jit(solution)/shard_map/all_gather | solution.py:11
  10.1 113.6 %copy-start.1 = (f32[4,128,128]{2,1,0:T(8,128)S(1)}, f32[4,128,128]{2,1,0:T(8,128)}, u32[]{:S(2)}) copy-start(f32[4,128,128]{2,1,0:T(8,128)} %fusion.14) | copy-start | bytes 786436
  10.1 197.4 %all-gather.4.cloned.1.call-start = ((), (), s32[]{:S(2)}) async-start(), calls=%async_computation.1 | async-start | bytes 4259840 | tf_op jit(solution)/shard_map/all_gather | solution.py:50
  10.9 257.5 %reduce-scatter.2.cloned.1.call-start = ((), (), s32[]{:S(2)}) async-start(), calls=%async_computation.2 | async-start | bytes 4718592 | tf_op jit(solution)/shard_map/reduce_scatter | solution.py:53
Sparse Core Ops, SparseCore 0:
  10.7 111.8 all-gather.5
  125.9 81.5 all-gather.3
  214.3 54.0 reduce-scatter.1
where the time goes:
time: 277 us; the launch traced here: 275 us
  waiting for transfers between devices  246 us (89%)
  between operations  13.2 us (5%)
  matrix products  11.4 us (4%)
    all_gather x1, waiting for transfers between devices, prefix(): gathered = lax.all_gather(part, axis)  112 us
    all_gather x1, waiting for transfers between devices, on_device(): lax.all_gather(out_weight, 'ctx', axis=1, tiled=True)  79.9 us
    reduce_scatter x1, waiting for transfers between devices, on_device(): lax.psum_scatter(terms.astype(jnp.bfloat16), 'tp', scatter_dimension=0, t...  54.2 us
    dot_general x1, matrix products, on_device(): jnp.dot(normed, lax.all_gather(out_weight, 'ctx', axis=1, tiled=True), pr...  6.53 us
  transfers between devices with their start and end apart: 3, of which 3 were waited for; matrix products, arithmetic and copies ran while one was open for 2% of the time, Pallas kernels for 0%

commit v1 on v0

--- a/solution.py
+++ b/solution.py
@@ -4,6 +4,14 @@
 from jax.sharding import PartitionSpec as P
 
 HD = 128
+
+
+def spans_list(point):
+    axis_n = lax.axis_size("ctx")
+    arrivals = [axis_n if ix == 1 else 1 for ix in range(point.ndim)]
+    current_arr = jnp.tile(point, arrivals)
+    piece_next = lax.all_to_all(current_arr, "ctx", concat_axis=1, tiled=True, split_axis=1)
+    return piece_next
 
 
 def prefix(part, axis, combine, identity):
@@ -45,11 +53,7 @@
     attended = inter + intra
     normed = attended / jnp.sqrt(jnp.mean(attended * attended, axis=-1, keepdims=True) + 1e-06)
     normed = normed.astype(jnp.bfloat16).reshape(tok_rows, heads_here * head_dim)
-    terms = jnp.dot(
-        normed,
-        lax.all_gather(out_weight, "ctx", axis=1, tiled=True),
-        preferred_element_type=jnp.float32,
-    )
+    terms = jnp.dot(normed, spans_list(out_weight), preferred_element_type=jnp.float32)
     summed = lax.psum_scatter(terms.astype(jnp.bfloat16), "tp", scatter_dimension=0, tiled=True)
     return summed
 

time: 277 us -> 311 us (1.12)
  waiting for transfers between devices: 246 us -> 263 us
  starting transfers between devices: 0.08 us -> 15.1 us
    all_gather x1 -> x0, waiting for transfers between devices: 79.9 us -> none  [on_device(): lax.all_gather(out_weight, 'ctx', axis=1, tiled=True)]
    reduce_scatter x1, waiting for transfers between devices: 54.2 us -> 118 us  [on_device(): lax.psum_scatter(terms.astype(jnp.bfloat16), 'tp', scatter_dimension=0, t...]
    all_gather x1, waiting for transfers between devices: 112 us -> 145 us  [prefix(): gathered = lax.all_gather(part, axis)]
    all_to_all x0 -> x1, starting transfers between devices: none -> 15 us  [spans_list(): lax.all_to_all(current_arr, 'ctx', concat_axis=1, tiled=True, split_axis=1)]
    another operation x1 -> x2, local copies, waits for them, and re-layouts: 1.26 us -> 4.63 us  [the longest x1 3.32 us: spans_list(): current_arr = jnp.tile(point, arrivals)]
  transfers between devices with their start and end apart: 3 -> 3, of which waited for: 3 -> 2; matrix products, arithmetic and copies ran while one was open for 2% -> 2% of each run, Pallas kernels for 0% -> 0%
where the time goes in v1:
time: 311 us; the launch traced here: 309 us
  waiting for transfers between devices  263 us (85%)
  starting transfers between devices  15.1 us (5%)
  between operations  13.5 us (4%)
  matrix products  11.4 us (4%)
  local copies, waits for them, and re-layouts  4.66 us (1%)
    all_gather x1, waiting for transfers between devices, prefix(): gathered = lax.all_gather(part, axis)  145 us
    reduce_scatter x1, waiting for transfers between devices, on_device(): lax.psum_scatter(terms.astype(jnp.bfloat16), 'tp', scatter_dimension=0, t...  118 us
    all_to_all x1, starting transfers between devices, spans_list(): lax.all_to_all(current_arr, 'ctx', concat_axis=1, tiled=True, split_axis=1)  15 us
    dot_general x1, matrix products, on_device(): jnp.dot(normed, spans_list(out_weight), preferred_element_type=jnp.float32)  6.54 us
  transfers between devices with their start and end apart: 3, of which 2 were waited for; matrix products, arithmetic and copies ran while one was open for 2% of the time, Pallas kernels for 0%

profile of v1, /device:TPU:1, one launch (start us, length us, event | category | flops | bytes accessed | tf_op | source)
XLA Modules:
  0.0 309.2 jit_solution(3703349121056326130)
XLA Ops:
  6.5 0.0 copy-start
  6.5 0.0 all-gather.3.cloned.1.call-start
  6.5 1.3 copy.24
  7.9 2.1 fusion.8
  10.0 0.0 all-gather.3.cloned.1.call-update
  10.0 3.3 %tile.2 = bf16[512,64,64]{0,2,1:T(8,128)(2,1)} broadcast(bf16[512,64]{0,1:T(8,128)(2,1)} %param.9), dimensions={0,2} | broadcast | bytes 4259840 | tf_op jit(solution)/shard_map/tile | solution.py:12
  13.3 15.0 %all-to-all-start = ((bf16[512,64,64]{0,2,1:T(8,128)(2,1)}), bf16[512,64,64]{0,2,1:T(8,128)(2,1)}, u32[]{:S(2)}, u32[]{:S(2)}) async-start(bf16[512,64,64]{0,2,1:T(8,128)(2,1)} %tile.2), calls=%async_computation | async-start | bytes 8388608 | tf_op jit(solution)/shard_map/all_to_all | solution.py:13
  28.3 0.0 copy-start.1
  28.3 0.0 reduce-scatter.2.cloned.1.call-start
  28.4 0.1 iota_compare_fusion
  28.5 144.9 %all-gather.3.cloned.1.call-done = f32[256,128,128]{2,1,0:T(8,128)} async-done(((f32[4,128,128]{2,1,0:T(8,128)}), f32[256,128,128]{2,1,0:T(8,128)}) %all-gather.3.cloned.1.call-update) | async-done | bytes 16777232 | tf_op jit(solution)/shard_map/all_gather | solution.py:19
  173.4 1.0 while.10
  173.4 1.0 bitcast_add_fusion.2
  174.5 0.0 copy-done
  174.5 0.0 copy-done.1
  174.5 0.3 fusion.6
  174.8 2.4 multiply_reduce_fusion
  177.3 0.1 divide_convert_fusion
  177.4 0.0 all-to-all-done
  177.4 6.5 %convolution_convert_fusion = bf16[512,4096]{1,0:T(8,128)(2,1)} fusion(bf16[512,512]{0,1:T(8,128)(2,1)S(1)} %bitcast.56, bf16[512,4096]{0,1:T(8,128)(2,1)} %bitcast.7), kind=kOutput, calls=%fused_computation.1 | convolution fusion | flops 2149580800 | bytes 8912896 | tf_op jit(solution)/shard_map/dot_general | solution.py:56
  183.9 0.0 reduce-scatter.2.cloned.1.call-update
  184.0 118.4 %reduce-scatter.2.cloned.1.call-done = bf16[64,4096]{1,0:T(8,128)(2,1)} async-done(((bf16[512,4096]{1,0:T(8,128)(2,1)}), bf16[64,4096]{1,0:T(8,128)(2,1)}) %reduce-scatter.2.cloned.1.call-update) | async-done | bytes 524304 | tf_op jit(solution)/shard_map/reduce_scatter | solution.py:57
  (2 shorter events, 0.0 us)
Async XLA Ops:
  6.5 167.9 %copy-start = (bf16[512,512]{1,0:T(8,128)(2,1)S(1)}, bf16[512,512]{1,0:T(8,128)(2,1)}, u32[]{:S(2)}) copy-start(bf16[512,512]{1,0:T(8,128)(2,1)} %param.6) | copy-start | bytes 1572868
  6.5 166.8 %all-gather.3.cloned.1.call-start = ((), (), s32[]{:S(2)}) async-start(), calls=%async_computation.3 | async-start | bytes 17039360 | tf_op jit(solution)/shard_map/all_gather | solution.py:19
  13.3 164.1 %all-to-all-start = ((bf16[512,64,64]{0,2,1:T(8,128)(2,1)}), bf16[512,64,64]{0,2,1:T(8,128)(2,1)}, u32[]{:S(2)}, u32[]{:S(2)}) async-start(bf16[512,64,64]{0,2,1:T(8,128)(2,1)} %tile.2), calls=%async_computation | async-start | bytes 8388608 | tf_op jit(solution)/shard_map/all_to_all | solution.py:13
  28.3 146.1 %copy-start.1 = (f32[4,128,128]{2,1,0:T(8,128)S(1)}, f32[4,128,128]{2,1,0:T(8,128)}, u32[]{:S(2)}) copy-start(f32[4,128,128]{2,1,0:T(8,128)} %fusion.8) | copy-start | bytes 786436
  28.3 274.0 %reduce-scatter.2.cloned.1.call-start = ((), (), s32[]{:S(2)}) async-start(), calls=%async_computation.2 | async-start | bytes 4718592 | tf_op jit(solution)/shard_map/reduce_scatter | solution.py:57
Sparse Core Ops, SparseCore 0:
  10.7 162.6 all-gather.2
  184.1 118.2 reduce-scatter.1
